TPU v7x, 256 devices: a whole 4x4x8 slice. The times are simulated.
256 devices in a mesh: seq: 32 (over y, z), head: 8 (over x, core).
Axes of the slice: x: 4, y: 4, z: 8, core: 2. Of those that a mesh axis runs over, the one named last changes fastest.
Arguments:
- teacher_query: bfloat16 [4096, 4096], P('seq', 'head'), may hold values from -20 to 20
- teacher_key: bfloat16 [4096, 4096], P('seq', 'head'), may hold values from -20 to 20
- student_query: bfloat16 [4096, 2048], P('seq', 'head'), may hold values from -20 to 20
- student_key: bfloat16 [4096, 2048], P('seq', 'head'), may hold values from -20 to 20
- doc_ids: int32 [4096], P('seq'), may hold values from 0 to 15, never falling along the last dimension, each value on 1 to 3072 neighbouring positions
Outputs:
- kl_loss: float32 [], replicated
- grad_query: bfloat16 [4096, 2048], P('seq', 'head')
- grad_key: bfloat16 [4096, 2048], P('seq', 'head')
Inputs may be any that keep to these rules, and one draw needn't show every extreme that they name: `doc_ids`: ids never fall along the positions; every document is a run of at most 3072 positions and one has exactly 3072.
All inputs are finite; a program needn't handle non-finite values.
Results may differ from a plain program's by a relative error of at most 0.009.
Values may be sent and summed in bfloat16 or wider, within the bound.
No kernel may reach another device: no remote copies, remote signals or barrier semaphores. Data moves between devices by JAX's collectives and lax.ppermute only.
A program may use at most 64 MiB of HBM per device.

v0:
```python
import math

import jax
import jax.numpy as jnp
from jax import lax
from jax.sharding import PartitionSpec as P

HDIM = 128
TDIM = 256


NEG = -1e30


def pair_mask(query_pos, query_doc, key_pos, key_doc):
    return (query_doc[:, None] == key_doc[None, :]) & (key_pos[None, :] <= query_pos[:, None])


def stacked(first_rows, second_rows, heads, head_size):
    return jnp.stack([first_rows, second_rows]).reshape(2, first_rows.shape[0], heads, head_size)


def split_norms(values):
    high_part = lax.optimization_barrier(values.astype(jnp.bfloat16))
    low_part = lax.optimization_barrier(
        (values - high_part.astype(jnp.float32)).astype(jnp.bfloat16)
    )
    return (high_part, low_part)


def in_blocks(step_fn, carried, fragment):
    length = fragment[0].shape[0]
    pieces = tuple((member.reshape((length // 512, 512) + member.shape[1:]) for member in fragment))

    def inner(state, items):
        blocks, number = items
        return (step_fn(state, blocks, number * 512), None)

    carried, unused = lax.scan(inner, carried, (pieces, jnp.arange(length // 512, dtype=jnp.int32)))
    return carried


def per_device(teacher_query, teacher_key, student_query, student_key, doc_ids):
    num_rows = teacher_query.shape[0]
    width = student_query.shape[1]
    heads = width // HDIM
    teach_factor = 1.0 / math.sqrt(TDIM)
    pupil_factor = 1.0 / math.sqrt(HDIM)
    seq_count = lax.axis_size("seq")
    seq_index = lax.axis_index("seq")
    first_pos = seq_index * num_rows
    my_pos = first_pos + jnp.arange(num_rows, dtype=jnp.int32)
    my_doc = doc_ids.astype(jnp.float32)
    teach = stacked(teacher_query, teacher_key, heads, TDIM)
    pupil = stacked(student_query, student_key, heads, HDIM)
    doc_wire = doc_ids.astype(jnp.bfloat16)

    def scores_with(other_teach, other_pupil):
        teacher_score = (
            jnp.einsum("rihd,rjhd->rhij", teach, other_teach, preferred_element_type=jnp.float32)
            * teach_factor
        )
        student_score = (
            jnp.einsum("rihd,rjhd->rhij", pupil, other_pupil, preferred_element_type=jnp.float32)
            * pupil_factor
        )
        return (teacher_score, student_score)

    def first_step(state, fragment, offset):
        frag_tq, frag_tk, frag_sq, frag_sk, frag_doc = fragment
        length = frag_tq.shape[0]
        key_pos = offset + jnp.arange(length, dtype=jnp.int32)
        key_doc = frag_doc.astype(jnp.float32)
        teacher_score, student_score = scores_with(
            stacked(frag_tq, frag_tk, heads, TDIM), stacked(frag_sq, frag_sk, heads, HDIM)
        )
        visible = pair_mask(my_pos, my_doc, key_pos, key_doc)
        top_t, sum_t, cross, top_s, sum_s = state
        new_t = jnp.maximum(top_t, jnp.max(jnp.where(visible, teacher_score, NEG), axis=-1))
        new_s = jnp.maximum(top_s, jnp.max(jnp.where(visible, student_score, NEG), axis=-1))
        weight_t = jnp.where(visible, jnp.exp(teacher_score - new_t[..., None]), 0.0)
        weight_s = jnp.where(visible, jnp.exp(student_score - new_s[..., None]), 0.0)
        decay_t = jnp.exp(top_t - new_t)
        decay_s = jnp.exp(top_s - new_s)
        return (
            new_t,
            sum_t * decay_t + jnp.sum(weight_t, axis=-1),
            cross * decay_t + jnp.sum(weight_t * (teacher_score - student_score), axis=-1),
            new_s,
            sum_s * decay_s + jnp.sum(weight_s, axis=-1),
        )

    zero_stat = jnp.zeros((2, heads, num_rows), jnp.float32)
    low_stat = jnp.full((2, heads, num_rows), NEG, jnp.float32)
    top_t, sum_t, cross, top_s, sum_s = in_blocks(
        first_step,
        (low_stat, zero_stat, zero_stat, low_stat, zero_stat),
        (
            lax.all_gather(teacher_query, "seq", axis=0, tiled=True),
            lax.all_gather(teacher_key, "seq", axis=0, tiled=True),
            lax.all_gather(student_query, "seq", axis=0, tiled=True),
            lax.all_gather(student_key, "seq", axis=0, tiled=True),
            lax.all_gather(doc_wire, "seq", axis=0, tiled=True),
        ),
    )
    lse_t = top_t + jnp.log(sum_t)
    lse_s = top_s + jnp.log(sum_s)
    row_kl = cross / sum_t - lse_t + lse_s
    total_kl = lax.psum(jnp.sum(row_kl), ("seq", "head"))
    kl_loss = total_kl / (2.0 * num_rows * seq_count * heads * lax.axis_size("head"))
    high_part, low_part = split_norms(jnp.stack([lse_t, lse_s]))
    norms = high_part.astype(jnp.float32) + low_part.astype(jnp.float32)
    my_norm_t = norms[0]
    my_norm_s = norms[1]
    empty_grad = jnp.zeros((2, num_rows, heads, HDIM), jnp.float32)
    wire_norms = jnp.moveaxis(jnp.stack([high_part, low_part]), -1, 0)

    def second_step(grad_sum, fragment, offset):
        frag_tq, frag_tk, frag_sq, frag_sk, frag_doc, frag_norm = fragment
        length = frag_tq.shape[0]
        key_pos = offset + jnp.arange(length, dtype=jnp.int32)
        key_doc = frag_doc.astype(jnp.float32)
        frag_pupil = stacked(frag_sq, frag_sk, heads, HDIM)
        teacher_score, student_score = scores_with(
            stacked(frag_tq, frag_tk, heads, TDIM), frag_pupil
        )
        frag_sum = frag_norm[:, 0].astype(jnp.float32) + frag_norm[:, 1].astype(jnp.float32)
        frag_lse = jnp.transpose(frag_sum, (1, 2, 3, 0))
        query_vis = pair_mask(my_pos, my_doc, key_pos, key_doc)
        key_vis = pair_mask(key_pos, key_doc, my_pos, my_doc).T
        own_grad = jnp.where(
            query_vis,
            jnp.exp(student_score - my_norm_s[..., None])
            - jnp.exp(teacher_score - my_norm_t[..., None]),
            0.0,
        ).astype(jnp.bfloat16)
        their_grad = jnp.where(
            key_vis,
            jnp.exp(student_score - frag_lse[1][:, :, None, :])
            - jnp.exp(teacher_score - frag_lse[0][:, :, None, :]),
            0.0,
        ).astype(jnp.bfloat16)
        grad_new = grad_sum + jnp.einsum(
            "rhij,rjhd->rihd", own_grad, frag_pupil, preferred_element_type=jnp.float32
        )
        return grad_new + jnp.einsum(
            "rhij,rjhd->rihd", their_grad, frag_pupil, preferred_element_type=jnp.float32
        )

    grad_total = in_blocks(
        second_step,
        empty_grad,
        (
            lax.all_gather(teacher_query, "seq", axis=0, tiled=True),
            lax.all_gather(teacher_key, "seq", axis=0, tiled=True),
            lax.all_gather(student_query, "seq", axis=0, tiled=True),
            lax.all_gather(student_key, "seq", axis=0, tiled=True),
            lax.all_gather(doc_wire, "seq", axis=0, tiled=True),
            lax.all_gather(wire_norms, "seq", axis=0, tiled=True),
        ),
    )
    grad_query = grad_total[0].reshape(num_rows, width).astype(jnp.bfloat16)
    grad_key = grad_total[1].reshape(num_rows, width).astype(jnp.bfloat16)
    return (kl_loss, grad_query, grad_key)


def solution(mesh):
    in_specs = (P("seq", "head"), P("seq", "head"), P("seq", "head"), P("seq", "head"), P("seq"))
    out_specs = (P(), P("seq", "head"), P("seq", "head"))
    return jax.shard_map(
        per_device, mesh=mesh, in_specs=in_specs, out_specs=out_specs, check_vma=False
    )
```

profile of v0, /device:TPU:32, one launch (start us, length us, event | category | flops | bytes accessed | tf_op | source)
XLA Modules:
  0.0 586.5 jit_solution(14569033248762674952)
XLA Ops:
  14.0 1.2 convert_bitcast_fusion
  15.2 40.2 %all-gather = bf16[32,1,128]{2,1,0:T(2,128)(2,1)S(1)} all-gather(bf16[1,1,128]{2,1,0:T(2,128)(2,1)S(1)} %get-tuple-element.456), channel_id=1, replica_groups=mesh['seq'=32,'head'=8] {'seq'}, dimensions={0}, use_global_device_ids=true | all-gather | bytes 8448 | tf_op jit(solution)/shard_map/all_gather | solution.py:103
  55.9 34.3 %all-gather.10.cloned.1.call-done = bf16[4096,256]{1,0:T(8,128)(2,1)} async-done(((bf16[128,256]{1,0:T(8,128)(2,1)}), bf16[4096,256]{1,0:T(8,128)(2,1)}) %all-gather.10.cloned.1.call-update) | async-done | bytes 2097168 | tf_op jit(solution)/shard_map/all_gather | solution.py:101
  90.2 3.9 copy.69
  94.1 73.9 %all-gather.12.cloned.1.call-done = bf16[4096,256]{1,0:T(8,128)(2,1)} async-done(((bf16[128,256]{1,0:T(8,128)(2,1)}), bf16[4096,256]{1,0:T(8,128)(2,1)}) %all-gather.12.cloned.1.call-update) | async-done | bytes 2097168 | tf_op jit(solution)/shard_map/all_gather | solution.py:102
  168.0 3.9 copy.70
  171.9 78.9 %all-gather.6.cloned.1.call-done = bf16[4096,512]{1,0:T(8,128)(2,1)} async-done(((bf16[128,512]{1,0:T(8,128)(2,1)}), bf16[4096,512]{1,0:T(8,128)(2,1)}) %all-gather.6.cloned.1.call-update) | async-done | bytes 4194320 | tf_op jit(solution)/shard_map/all_gather | solution.py:99
  250.8 6.5 %copy.66 = bf16[8,512,512]{1,2,0:T(8,128)(2,1)} copy(bf16[8,512,512]{2,1,0:T(8,128)(2,1)} %bitcast.138) | data formatting | bytes 8388608
  257.3 75.0 %all-gather.8.cloned.1.call-done = bf16[4096,512]{1,0:T(8,128)(2,1)} async-done(((bf16[128,512]{1,0:T(8,128)(2,1)}), bf16[4096,512]{1,0:T(8,128)(2,1)}) %all-gather.8.cloned.1.call-update) | async-done | bytes 4194320 | tf_op jit(solution)/shard_map/all_gather | solution.py:100
  332.3 6.5 %copy.67 = bf16[8,512,512]{1,2,0:T(8,128)(2,1)} copy(bf16[8,512,512]{2,1,0:T(8,128)(2,1)} %bitcast.139) | data formatting | bytes 8388608
  338.8 63.4 %while.30 = (s32[]{:T(128)}, f32[2,2,128]{2,1,0:T(2,128)S(1)}, f32[2,2,128]{2,1,0:T(2,128)S(1)}, f32[2,2,128]{2,1,0:T(2,128)S(1)}, f32[2,2,128]{2,1,0:T(2,128)S(...) while((s32[]{:T(128)}, f32[2,2,128]{2,1,0:T(2,128)S(1)}, ...), condition=%wide.region_6.7_spmd.clone, body=%wide.region_0.6_spmd.clone.sunk | while | flops 206249088 | bytes 13769461 | solution.py:39
  339.9 1.1 constant_dynamic-slice_fusion.15
  347.8 1.1 constant_dynamic-slice_fusion.15
  402.8 74.5 %psum.7 = f32[]{:T(128)} all-reduce(f32[]{:T(128)} %get-tuple-element.454), channel_id=1, replica_groups=mesh['seq'=32,'head'=8] {'seq','head'}, use_global_device_ids=true, to_apply=%region_8.9 | all-reduce | flops 1 | bytes 8 | tf_op jit(solution)/shard_map/psum | solution.py:109
  477.4 38.2 %all_gather.28 = bf16[4096,2,2,2,2]{0,4,3,2,1:T(2,128)(2,1)S(1)} all-gather(bf16[128,2,2,2,2]{0,4,3,2,1:T(2,128)(2,1)S(1)} %maximum_bitcast_fusion), channel_id=1, replica_groups=mesh['seq'=32,'head'=8] {'seq'}, dimensions={0}, use_global_device_ids=true | all-gather | bytes 135168 | tf_op jit(solution)/shard_map/all_gather | solution.py:159
  516.1 60.5 %while.31 = (s32[]{:T(128)}, f32[2,128,2,128]{1,3,2,0:T(8,128)S(1)}, bf16[8,512,256]{1,2,0:T(8,128)(2,1)}, bf16[8,512,256]{1,2,0:T(8,128)(2,1)}, f32[128]{0:T(12...) while((s32[]{:T(128)}, ...), condition=%wide.region_10.11_spmd.clone, body=%wide.region_9.10_spmd.clone.sunk | while | flops 340079744 | bytes 17038056 | solution.py:39
  517.3 1.3 constant_dynamic-slice_fusion.19
  519.6 1.2 dynamic_slice.89
  524.8 1.3 constant_dynamic-slice_fusion.19
  527.1 1.2 dynamic_slice.89
  532.4 1.3 constant_dynamic-slice_fusion.19
  534.7 1.2 dynamic_slice.89
  540.0 1.3 constant_dynamic-slice_fusion.19
  542.2 1.2 dynamic_slice.89
  547.5 1.3 constant_dynamic-slice_fusion.19
  549.8 1.2 dynamic_slice.89
  555.1 1.3 constant_dynamic-slice_fusion.19
  557.4 1.2 dynamic_slice.89
  562.6 1.3 constant_dynamic-slice_fusion.19
  564.9 1.2 dynamic_slice.89
  570.2 1.3 constant_dynamic-slice_fusion.19
  572.5 1.2 dynamic_slice.89
  (299 shorter events, 100.2 us)
Async XLA Ops:
  7.2 83.1 %all-gather.10.cloned.1.call-start = ((), (), s32[]{:S(2)}) async-start(), calls=%async_computation.2 | async-start | bytes 2162688 | tf_op jit(solution)/shard_map/all_gather | solution.py:101
  7.9 160.1 %all-gather.12.cloned.1.call-start = ((), (), s32[]{:S(2)}) async-start(), calls=%async_computation.3 | async-start | bytes 2162688 | tf_op jit(solution)/shard_map/all_gather | solution.py:102
  8.6 242.1 %all-gather.6.cloned.1.call-start = ((), (), s32[]{:S(2)}) async-start(), calls=%async_computation | async-start | bytes 4325376 | tf_op jit(solution)/shard_map/all_gather | solution.py:99
  9.4 322.9 %all-gather.8.cloned.1.call-start = ((), (), s32[]{:S(2)}) async-start(), calls=%async_computation.1 | async-start | bytes 4325376 | tf_op jit(solution)/shard_map/all_gather | solution.py:100
Sparse Core Ops, SparseCore 0:
  10.6 79.5 all-gather.9
  92.8 75.1 all-gather.11
  170.6 80.1 all-gather.5
  253.2 79.0 all-gather.7
where the time goes:
time: 589 us; the launch traced here: 586 us
  waiting for transfers between devices  265 us (45%)
  blocking collectives  153 us (26%)
  local copies, waits for them, and re-layouts  93.5 us (16%)
  matrix products  25.3 us (4%)
  other arithmetic  22.8 us (4%)
  between operations  15.7 us (3%)
  loops' own time  11.5 us (2%)
    all_gather x1, waiting for transfers between devices, per_device(): lax.all_gather(teacher_query, 'seq', axis=0, tiled=True)  78.9 us
    all_gather x1, waiting for transfers between devices, per_device(): lax.all_gather(teacher_key, 'seq', axis=0, tiled=True)  75 us
    psum x1, blocking collectives, per_device(): total_kl = lax.psum(jnp.sum(row_kl), ('seq', 'head'))  74.5 us
    all_gather x1, waiting for transfers between devices, per_device(): lax.all_gather(student_key, 'seq', axis=0, tiled=True)  73.9 us
    dynamic_slice x64, local copies, waits for them, and re-layouts, in_blocks(): lax.scan(inner, carried, (pieces, jnp.arange(length // 512, dtype=jnp.int...  66 us
    all_gather x1, blocking collectives, per_device(): lax.all_gather(doc_wire, 'seq', axis=0, tiled=True)  40.2 us
    all_gather x1, blocking collectives, per_device(): lax.all_gather(wire_norms, 'seq', axis=0, tiled=True)  38.2 us
    all_gather x1, waiting for transfers between devices, per_device(): lax.all_gather(student_query, 'seq', axis=0, tiled=True)  34.3 us
  transfers between devices with their start and end apart: 4, of which 4 were waited for; matrix products, arithmetic and copies ran while one was open for 3% of the time, Pallas kernels for 0%

commit v1 on v0

v1 whole, which is shorter than its diff:
```python
import functools
import math

import jax
import jax.numpy as jnp
from jax import lax
from jax.experimental import pallas as pl
from jax.experimental.pallas import tpu as pltpu
from jax.sharding import PartitionSpec as P

HDIM = 128
TDIM = 256
WIDE = TDIM + HDIM
NY, NZ, NX = 4, 8, 4
ROWS = 128
BLOCK = 512
TILE = 256
TOKENS = 4096
TILES = TOKENS // TILE
NEG = -1e30
LOG2E = 1.4426950408889634
LN2 = 0.6931471805599453
KT = LOG2E / math.sqrt(TDIM)
KS = LOG2E / math.sqrt(HDIM)
VMEM_LIMIT = 48 * 1024 * 1024
F32 = jnp.float32
BF16 = jnp.bfloat16
AXES = ("seq", "head")
ALL = pl.BlockSpec(memory_space=pltpu.VMEM)
SMEM = pl.BlockSpec(memory_space=pltpu.SMEM)
ANY = pl.BlockSpec(memory_space=pl.ANY)


def device(y, z, x, core):
    return (y * NZ + z) * (2 * NX) + x * 2 + core


def pairs_of(move):
    pairs = []
    for y in range(NY):
        for z in range(NZ):
            for x in range(NX):
                for core in range(2):
                    pairs.append((device(y, z, x, core), device(*move(y, z, x, core))))
    return pairs


def spread_pairs(j):
    return pairs_of(lambda y, z, x, c: (y, 4 * c + (z % 4 + j) % 4, x, z // 4))


def collect_pairs(j):
    return [(target, source) for source, target in spread_pairs(j)]


def y_pairs(step):
    return pairs_of(lambda y, z, x, c: ((y + step) % NY, z, x, c))


def x_pairs(bit):
    return pairs_of(lambda y, z, x, c: (y, z, x ^ bit, c))


CORE_PAIRS = pairs_of(lambda y, z, x, c: (y, z, x, 1 - c))


def params():
    return pltpu.CompilerParams(vmem_limit_bytes=VMEM_LIMIT)


def nt_dot(left, right):
    return lax.dot_general(left, right, (((1,), (1,)), ((), ())), preferred_element_type=F32)


def send_kernel(place, tq, tk, sq, sk, doc, o0, o1, o2, o3, held):
    below = doc[...] < lax.broadcasted_iota(jnp.int32, (128, ROWS), 0)
    counts = nt_dot(jnp.ones((16, ROWS), BF16), below.astype(F32).astype(BF16))
    for m, (teach, pupil) in enumerate(((tq, sq), (tq, sq), (tk, sk), (tk, sk))):
        h = m % 2
        held[m, 0:ROWS, 0:TDIM] = teach[:, h * TDIM:(h + 1) * TDIM]
        held[m, 0:ROWS, TDIM:WIDE] = pupil[:, h * HDIM:(h + 1) * HDIM]
        held[m, ROWS:ROWS + 16, 0:128] = counts.astype(BF16)
        held[m, ROWS:ROWS + 16, 128:WIDE] = jnp.zeros((16, 256), BF16)
    b = place[1] % 4
    for j, out in enumerate((o0, o1, o2, o3)):
        out[...] = held[(b + j) % 4]


def pack_kernel(place, r0, r1, r2, r3, out):
    m = place[1] % 4
    for j, got in enumerate((r0, r1, r2, r3)):
        b = (m - j + 4) % 4
        out[pl.ds(pl.multiple_of(b * ROWS, ROWS), ROWS), :] = got[0:ROWS, :]
    out[BLOCK:BLOCK + 16, 0:128] = r0[ROWS:ROWS + 16, 0:128] + r1[ROWS:ROWS + 16, 0:128]
    out[BLOCK:BLOCK + 16, 128:256] = r2[ROWS:ROWS + 16, 0:128] + r3[ROWS:ROWS + 16, 0:128]
    out[BLOCK:BLOCK + 16, 256:WIDE] = jnp.zeros((16, 128), BF16)


def assemble(place, parts, rows, counts, sems):
    y, core = place[0], place[2]
    copies = []
    for n, part in enumerate(parts):
        i, other = n // 2, n % 2
        from_core = core if other == 0 else 1 - core
        r = ((y - i + NY) % NY) * 2 + from_core
        copies.append(
            pltpu.make_async_copy(
                part.at[pl.ds(0, BLOCK)],
                rows.at[pl.ds(pl.multiple_of(r * BLOCK, BLOCK), BLOCK)],
                sems.at[n],
            )
        )
        copies.append(
            pltpu.make_async_copy(part.at[pl.ds(BLOCK, 16)], counts.at[n], sems.at[8 + n])
        )
    for copy in copies:
        copy.start()
    for copy in copies:
        copy.wait()
    total = jnp.zeros((16, 128), F32)
    for n in range(8):
        total = total + counts[n, :, 0:128].astype(F32) + counts[n, :, 128:256].astype(F32)
    return total[0:1]


def start_of(bounds, position):
    return jnp.max(jnp.where(bounds <= position, bounds, 0.0))


def end_of(bounds, position):
    return jnp.min(jnp.where(bounds > position, bounds, float(TOKENS)))


def tile_rows(t):
    return pl.ds(pl.multiple_of(t * TILE, TILE), TILE)


def folded(values):
    return values.reshape(TILE // 8, 8, TILE)


def norm_kernel(place, *refs):
    parts, out = refs[:8], refs[8]
    rows, counts, scores_t, scores_s, sems = refs[9:]
    bounds = assemble(place, parts, rows, counts, sems)
    r = place[0] * 2 + place[2]
    bounds_down = jnp.transpose(jnp.broadcast_to(bounds, (128, 128)))[0:16, 0:1]
    out[...] = jnp.zeros_like(out)
    for half in range(2):
        t = r if half == 0 else TILES - 1 - r
        first = t * TILE
        mine_t = rows[tile_rows(t), 0:TDIM]
        mine_s = rows[tile_rows(t), TDIM:WIDE]
        low = start_of(bounds, first.astype(F32)).astype(jnp.int32)
        high = start_of(bounds, (first + TILE - 1).astype(F32)).astype(jnp.int32)
        my_pos = first + lax.broadcasted_iota(jnp.int32, (1, TILE), 1)
        my_start = jnp.max(
            jnp.where(bounds_down <= my_pos.astype(F32), bounds_down, 0.0), axis=0, keepdims=True
        ).astype(jnp.int32)

        def score(c, tops, masked):
            t_tile = nt_dot(rows[tile_rows(c), 0:TDIM], mine_t) * KT
            s_tile = nt_dot(rows[tile_rows(c), TDIM:WIDE], mine_s) * KS
            if masked:
                pos = c * TILE + lax.broadcasted_iota(jnp.int32, (TILE, TILE), 0)
                seen = (pos <= my_pos) & (pos >= my_start)
                t_tile = jnp.where(seen, t_tile, NEG)
                s_tile = jnp.where(seen, s_tile, NEG)
            scores_t[tile_rows(c), :] = t_tile
            scores_s[tile_rows(c), :] = s_tile
            return (
                jnp.maximum(tops[0], jnp.max(folded(t_tile), axis=0)),
                jnp.maximum(tops[1], jnp.max(folded(s_tile), axis=0)),
            )

        from_tile = low // TILE
        plain_tile = jnp.minimum((high + TILE - 1) // TILE, t)
        tops = (jnp.full((8, TILE), NEG, F32), jnp.full((8, TILE), NEG, F32))
        tops = lax.fori_loop(from_tile, plain_tile, functools.partial(score, masked=True), tops)
        tops = lax.fori_loop(plain_tile, t, functools.partial(score, masked=False), tops)
        tops = score(t, tops, True)
        top_t = jnp.max(tops[0], axis=0, keepdims=True)
        top_s = jnp.max(tops[1], axis=0, keepdims=True)

        def add(c, sums):
            sum_t, sum_s, cross = sums
            t_tile = scores_t[tile_rows(c), :]
            s_tile = scores_s[tile_rows(c), :]
            p = jnp.exp2(t_tile - top_t)
            q = jnp.exp2(s_tile - top_s)
            return (
                sum_t + jnp.sum(folded(p), axis=0),
                sum_s + jnp.sum(folded(q), axis=0),
                cross + jnp.sum(folded(p * (t_tile - s_tile)), axis=0),
            )

        zero = jnp.zeros((8, TILE), F32)
        sums = lax.fori_loop(from_tile, t + 1, add, (zero, zero, zero))
        sum_t, sum_s, cross = (jnp.sum(v, axis=0, keepdims=True) for v in sums)
        lse_t = top_t * LN2 + jnp.log(sum_t)
        lse_s = top_s * LN2 + jnp.log(sum_s)
        row_kl = cross * LN2 / sum_t - lse_t + lse_s
        for k, lse in enumerate((lse_t, lse_s)):
            high_part = lse.astype(BF16).astype(F32)
            low_part = (lse - high_part).astype(BF16).astype(F32)
            out[2 * half + k:2 * half + k + 1, :] = (high_part + low_part) * LOG2E
        out[4 + half:5 + half, :] = row_kl


def grad_kernel(place, *refs):
    parts, packets, outs = refs[:8], refs[8:12], refs[12:16]
    rows, counts, norms, row_norm, acc, sems = refs[16:]
    bounds = assemble(place, parts, rows, counts, sems)
    y, core = place[0], place[2]
    r = y * 2 + core
    m = place[1] % 4
    kl = jnp.zeros((1, TILE), F32)
    for i, packet in enumerate(packets):
        for other in range(2):
            from_core = core if other == 0 else 1 - core
            from_r = ((y - i + NY) % NY) * 2 + from_core
            norms[from_r, 0:2, :] = packet[8 * other:8 * other + 2, :]
            norms[TILES - 1 - from_r, 0:2, :] = packet[8 * other + 2:8 * other + 4, :]
            kl = kl + packet[8 * other + 4:8 * other + 5, :] + packet[8 * other + 5:8 * other + 6, :]
    kl = kl[:, 0:128] + kl[:, 128:256]
    for half in range(2):
        t = 2 * r + half
        first = t * TILE
        mine_t = rows[tile_rows(t), 0:TDIM]
        mine_s = rows[tile_rows(t), TDIM:WIDE]
        for k in range(2):
            row_norm[k] = jnp.transpose(jnp.broadcast_to(norms[t, k:k + 1, :], (128, TILE)))
        my_pos = first + lax.broadcasted_iota(jnp.int32, (TILE, 1), 0)
        my_posf = my_pos.astype(F32)
        my_start = jnp.max(jnp.where(bounds <= my_posf, bounds, 0.0), axis=1, keepdims=True)
        my_end = jnp.min(jnp.where(bounds > my_posf, bounds, float(TOKENS)), axis=1, keepdims=True)
        my_start, my_end = my_start.astype(jnp.int32), my_end.astype(jnp.int32)
        start_low = start_of(bounds, first.astype(F32)).astype(jnp.int32)
        start_high = start_of(bounds, (first + TILE - 1).astype(F32)).astype(jnp.int32)
        end_low = end_of(bounds, first.astype(F32)).astype(jnp.int32)
        end_high = end_of(bounds, (first + TILE - 1).astype(F32)).astype(jnp.int32)
        acc[...] = jnp.zeros_like(acc)

        def step(c, unused, kind, masked):
            pupil = rows[tile_rows(c), TDIM:WIDE]
            t_tile = nt_dot(mine_t, rows[tile_rows(c), 0:TDIM]) * KT
            s_tile = nt_dot(mine_s, pupil) * KS
            mine = [jnp.concatenate([row_norm[k], row_norm[k]], axis=1) for k in range(2)]
            theirs = [norms[c, k:k + 1, :] for k in range(2)]
            pos = c * TILE + lax.broadcasted_iota(jnp.int32, (TILE, TILE), 1)
            if kind == "below":
                norm_t, norm_s = mine
            elif kind == "above":
                norm_t, norm_s = theirs
            else:
                own = pos <= my_pos
                norm_t, norm_s = (jnp.where(own, mine[k], theirs[k]) for k in range(2))
            weight = jnp.exp2(s_tile - norm_s) - jnp.exp2(t_tile - norm_t)
            if kind == "diagonal":
                weight = jnp.where(pos == my_pos, 2.0 * weight, weight)
            if masked:
                weight = jnp.where((pos >= my_start) & (pos < my_end), weight, 0.0)
            acc[...] += jnp.dot(weight.astype(BF16), pupil, preferred_element_type=F32)
            return unused

        def run(begin, stop, kind, masked):
            lax.fori_loop(begin, stop, functools.partial(step, kind=kind, masked=masked), 0)

        plain = jnp.minimum((start_high + TILE - 1) // TILE, t)
        run(start_low // TILE, plain, "below", True)
        run(plain, t, "below", False)
        step(t, 0, "diagonal", True)
        plain = jnp.maximum(end_low // TILE, t + 1)
        run(t + 1, plain, "above", False)
        run(plain, (end_high + TILE - 1) // TILE, "above", True)
        for q in range(2):
            b = 2 * half + q
            for j in range(4):

                @pl.when((m - j + 4) % 4 == b)
                def _():
                    outs[j][0:ROWS, :] = acc[q * ROWS:(q + 1) * ROWS, :].astype(BF16)

    high_part = kl.astype(BF16).astype(F32)
    mid_part = (kl - high_part).astype(BF16).astype(F32)
    low_part = (kl - high_part - mid_part).astype(BF16).astype(F32)
    line = lax.broadcasted_iota(jnp.int32, (16, 128), 0)
    tail = jnp.where(line == 0, high_part, jnp.where(line == 1, mid_part, jnp.where(line == 2, low_part, 0.0)))
    for j in range(4):
        outs[j][ROWS:ROWS + 16, :] = tail.astype(BF16)


def finish_kernel(place, g0, g1, g2, g3, grad_q, grad_k, kl_out, held):
    b = place[1] % 4
    kl = jnp.zeros((16, 128), F32)
    for j, got in enumerate((g0, g1, g2, g3)):
        held[(b + j) % 4] = got[0:ROWS, :]
        kl = kl + got[ROWS:ROWS + 16, :].astype(F32)
    for m in range(4):
        out = grad_q if m < 2 else grad_k
        h = m % 2
        out[:, h * HDIM:(h + 1) * HDIM] = held[m]
    kl_out[...] = kl[0:8]


def per_device(teacher_query, teacher_key, student_query, student_key, doc_ids):
    seq, head = lax.axis_index("seq"), lax.axis_index("head")
    place = jnp.stack([seq // NZ, seq % NZ, head % 2]).astype(jnp.int32)

    block = jax.ShapeDtypeStruct((ROWS + 16, WIDE), BF16)
    sends = pl.pallas_call(
        send_kernel,
        out_shape=[block] * 4,
        in_specs=[SMEM] + [ALL] * 5,
        out_specs=[ALL] * 4,
        scratch_shapes=[pltpu.VMEM((4, ROWS + 16, WIDE), BF16)],
        compiler_params=params(),
    )(place, teacher_query, teacher_key, student_query, student_key, doc_ids.reshape(1, ROWS))
    gots = [lax.ppermute(sends[j], AXES, spread_pairs(j)) for j in range(4)]
    own = pl.pallas_call(
        pack_kernel,
        out_shape=jax.ShapeDtypeStruct((BLOCK + 16, WIDE), BF16),
        in_specs=[SMEM] + [ALL] * 4,
        out_specs=ALL,
        compiler_params=params(),
    )(place, *gots)
    parts = []
    for step in range(4):
        part = own if step == 0 else lax.ppermute(own, AXES, y_pairs(step))
        parts += [part, lax.ppermute(part, AXES, CORE_PAIRS)]
    gathered = [
        pltpu.VMEM((TOKENS, WIDE), BF16),
        pltpu.VMEM((8, 16, WIDE), BF16),
    ]
    packet = pl.pallas_call(
        norm_kernel,
        out_shape=jax.ShapeDtypeStruct((8, TILE), F32),
        in_specs=[SMEM] + [ANY] * 8,
        out_specs=ALL,
        scratch_shapes=gathered
        + [
            pltpu.VMEM((TOKENS, TILE), F32),
            pltpu.VMEM((TOKENS, TILE), F32),
            pltpu.SemaphoreType.DMA((16,)),
        ],
        compiler_params=params(),
    )(place, *parts)
    both = jnp.concatenate([packet, lax.ppermute(packet, AXES, CORE_PAIRS)])
    packets = [both] + [lax.ppermute(both, AXES, y_pairs(step)) for step in (1, 2, 3)]
    grads = pl.pallas_call(
        grad_kernel,
        out_shape=[jax.ShapeDtypeStruct((ROWS + 16, HDIM), BF16)] * 4,
        in_specs=[SMEM] + [ANY] * 8 + [ALL] * 4,
        out_specs=[ALL] * 4,
        scratch_shapes=gathered
        + [
            pltpu.VMEM((TILES, 8, TILE), F32),
            pltpu.VMEM((2, TILE, 128), F32),
            pltpu.VMEM((TILE, HDIM), F32),
            pltpu.SemaphoreType.DMA((16,)),
        ],
        compiler_params=params(),
    )(place, *parts, *packets)
    backs = [lax.ppermute(grads[j], AXES, collect_pairs(j)) for j in range(4)]
    half_grad = jax.ShapeDtypeStruct((ROWS, 2 * HDIM), BF16)
    grad_query, grad_key, kl = pl.pallas_call(
        finish_kernel,
        out_shape=[half_grad, half_grad, jax.ShapeDtypeStruct((8, 128), F32)],
        in_specs=[SMEM] + [ALL] * 4,
        out_specs=[ALL] * 3,
        scratch_shapes=[pltpu.VMEM((4, ROWS, HDIM), BF16)],
        compiler_params=params(),
    )(place, *backs)
    for pairs in (x_pairs(1), x_pairs(2), CORE_PAIRS):
        kl = kl + lax.ppermute(kl, AXES, pairs)
    kl_loss = jnp.sum(kl) / (2.0 * TOKENS * 16)
    return (kl_loss, grad_query, grad_key)


def solution(mesh):
    in_specs = (P("seq", "head"), P("seq", "head"), P("seq", "head"), P("seq", "head"), P("seq"))
    out_specs = (P(), P("seq", "head"), P("seq", "head"))
    return jax.shard_map(
        per_device, mesh=mesh, in_specs=in_specs, out_specs=out_specs, check_vma=False
    )
```

time: 589 us -> 106 us (0.18)
  waiting for transfers between devices: 265 us -> 23.6 us
  blocking collectives: 153 us -> 0 us
  local copies, waits for them, and re-layouts: 93.5 us -> 3.38 us
  starting transfers between devices: 0.15 us -> 54.1 us
  matrix products: 25.3 us -> 0 us
  other arithmetic: 22.8 us -> 0.68 us
  Pallas kernels: 0 us -> 21.3 us
  between operations: 15.7 us -> 2.52 us
  loops' own time: 11.5 us -> 0 us
    all_gather x4 -> x0, waiting for transfers between devices: 262 us -> none  [the longest x1 78.9 us: per_device(): lax.all_gather(teacher_query, 'seq', axis=0, tiled=True)]
    all_gather x2 -> x0, blocking collectives: 78.4 us -> none  [the longest x1 40.2 us: per_device(): lax.all_gather(doc_wire, 'seq', axis=0, tiled=True)]
    psum x1 -> x0, blocking collectives: 74.5 us -> none  [per_device(): total_kl = lax.psum(jnp.sum(row_kl), ('seq', 'head'))]
    dynamic_slice x64 -> x0, local copies, waits for them, and re-layouts: 66 us -> none  [in_blocks(): lax.scan(inner, carried, (pieces, jnp.arange(length // 512, dtype=jnp.int...]
    ppermute x0 -> x22, starting transfers between devices: none -> 54.1 us  [the longest x4 19.1 us: per_device(): parts += [part, lax.ppermute(part, AXES, CORE_PAIRS)]]
    dot_general x48 -> x0, matrix products: 25.3 us -> none  [the longest x16 8.43 us: scores_with(): jnp.einsum('rihd,rjhd->rhij', teach, other_teach, preferred_element_type=...]
    ppermute x0 -> x22, waiting for transfers between devices: none -> 23.6 us  [the longest x4 7.58 us: per_device(): gots = [lax.ppermute(sends[j], AXES, spread_pairs(j)) for j in range(4)]]
    unnamed x10, local copies, waits for them, and re-layouts: 25 us -> 3.38 us
  transfers between devices with their start and end apart: 4 -> 22, of which waited for: 4 -> 12; matrix products, arithmetic and copies ran while one was open for 3% -> 0% of each run, Pallas kernels for 0% -> 0%
where the time goes in v1:
time: 106 us
  starting transfers between devices  54.1 us (51%)
  waiting for transfers between devices  23.6 us (22%)
  Pallas kernels  21.3 us (20%)
  local copies, waits for them, and re-layouts  3.38 us (3%)
  between operations  2.52 us (2%)
    ppermute x4, starting transfers between devices, per_device(): parts += [part, lax.ppermute(part, AXES, CORE_PAIRS)]  19.1 us
    pallas_call x1, Pallas kernels, per_device(): pl.pallas_call(grad_kernel, out_shape=[jax.ShapeDtypeStruct((ROWS + 16, H...  15 us
    ppermute x3, starting transfers between devices, per_device(): kl = kl + lax.ppermute(kl, AXES, pairs)  12.4 us
    ppermute x4, waiting for transfers between devices, per_device(): gots = [lax.ppermute(sends[j], AXES, spread_pairs(j)) for j in range(4)]  7.58 us
    ppermute x3, starting transfers between devices, per_device(): lax.ppermute(both, AXES, y_pairs(step))  7.08 us
    ppermute x3, waiting for transfers between devices, per_device(): kl = kl + lax.ppermute(kl, AXES, pairs)  6.16 us
    ppermute x4, starting transfers between devices, per_device(): gots = [lax.ppermute(sends[j], AXES, spread_pairs(j)) for j in range(4)]  6.04 us
    ppermute x4, starting transfers between devices, per_device(): backs = [lax.ppermute(grads[j], AXES, collect_pairs(j)) for j in range(4)]  5.57 us
  transfers between devices with their start and end apart: 22, of which 12 were waited for; matrix products, arithmetic and copies ran while one was open for 0% of the time, Pallas kernels for 0%

profile of v1, /device:TPU:32, one launch (start us, length us, event | category | flops | bytes accessed | tf_op | source)
XLA Modules:
  0.0 105.6 jit_solution(13645440884929055204)
XLA Ops:
  1.5 0.9 copy-done
  2.4 0.9 copy-done.1
  3.3 0.8 copy-done.3
  5.5 2.0 %collective-permute-start.1 = (bf16[144,384]{1,0:T(8,128)(2,1)S(1)}, bf16[144,384]{1,0:T(8,128)(2,1)S(1)}, u32[]{:S(2)}, u32[]{:S(2)}) collective-permute-start(bf16[144,384]{1,0:T(8,128)(2,1)S(1)} %get-tuple-element.15), channel_id=1, source_target_pairs={{0,8},{1,40},{2,10},{3,42},{4,12},{5,44},{6,14},{7,46},{8,16},{9,4... | collective-permute-start | bytes 331784 | tf_op jit(solution)/shard_map/ppermute | solution.py:319
  7.5 2.3 %collective-permute-start.2 = (bf16[144,384]{1,0:T(8,128)(2,1)S(1)}, bf16[144,384]{1,0:T(8,128)(2,1)S(1)}, u32[]{:S(2)}, u32[]{:S(2)}) collective-permute-start(bf16[144,384]{1,0:T(8,128)(2,1)S(1)} %get-tuple-element.16), channel_id=1, source_target_pairs={{0,16},{1,48},{2,18},{3,50},{4,20},{5,52},{6,22},{7,54},{8,24},{9,... | collective-permute-start | bytes 331784 | tf_op jit(solution)/shard_map/ppermute | solution.py:319
  9.8 1.1 %collective-permute-start.3 = (bf16[144,384]{1,0:T(8,128)(2,1)S(1)}, bf16[144,384]{1,0:T(8,128)(2,1)S(1)}, u32[]{:S(2)}, u32[]{:S(2)}) collective-permute-start(bf16[144,384]{1,0:T(8,128)(2,1)S(1)} %get-tuple-element.17), channel_id=1, source_target_pairs={{0,24},{1,56},{2,26},{3,58},{4,28},{5,60},{6,30},{7,62},{8,0},{9,3... | collective-permute-start | bytes 331784 | tf_op jit(solution)/shard_map/ppermute | solution.py:319
  10.9 5.9 %collective-permute-done.2.r2 = bf16[144,384]{1,0:T(8,128)(2,1)S(1)} collective-permute-done((bf16[144,384]{1,0:T(8,128)(2,1)S(1)}, bf16[144,384]{1,0:T(8,128)(2,1)S(1)}, u32[]{:S(2)}, u32[]{:S(2)}) %collective-permute-start.2) | collective-permute-done | bytes 110624 | tf_op jit(solution)/shard_map/ppermute | solution.py:319
  16.9 1.6 %collective-permute-done.3.r3 = bf16[144,384]{1,0:T(8,128)(2,1)S(1)} collective-permute-done((bf16[144,384]{1,0:T(8,128)(2,1)S(1)}, bf16[144,384]{1,0:T(8,128)(2,1)S(1)}, u32[]{:S(2)}, u32[]{:S(2)}) %collective-permute-start.3) | collective-permute-done | bytes 110624 | tf_op jit(solution)/shard_map/ppermute | solution.py:319
  19.1 1.6 %collective-permute-start.9 = (bf16[528,384]{1,0:T(8,128)(2,1)S(1)}, bf16[528,384]{1,0:T(8,128)(2,1)S(1)}, u32[]{:S(2)}, u32[]{:S(2)}) collective-permute-start(bf16[528,384]{1,0:T(8,128)(2,1)S(1)} %shard_map.77.refs_0_), channel_id=1, source_target_pairs={{0,192},{1,193},{2,194},{3,195},{4,196},{5,197},{6,198},{7,199},{8... | collective-permute-start | bytes 1216520 | tf_op jit(solution)/shard_map/ppermute | solution.py:329
  21.3 1.0 collective-permute-start.5
  22.3 6.2 %collective-permute-start.4 = (bf16[528,384]{1,0:T(8,128)(2,1)S(1)}, bf16[528,384]{1,0:T(8,128)(2,1)S(1)}, u32[]{:S(2)}, u32[]{:S(2)}) collective-permute-start(bf16[528,384]{1,0:T(8,128)(2,1)S(1)} %shard_map.77.refs_0_), channel_id=1, source_target_pairs={{0,1},{1,0},{2,3},{3,2},{4,5},{5,4},{6,7},{7,6},{8,9},{9,8},{10,11... | collective-permute-start | bytes 1216520 | tf_op jit(solution)/shard_map/ppermute | solution.py:330
  28.5 11.5 %collective-permute-start.10 = (bf16[528,384]{1,0:T(8,128)(2,1)S(1)}, bf16[528,384]{1,0:T(8,128)(2,1)S(1)}, u32[]{:S(2)}, u32[]{:S(2)}) collective-permute-start(bf16[528,384]{1,0:T(8,128)(2,1)S(1)} %collective-permute-done.9.refs_6_), channel_id=1, source_target_pairs={{0,1},{1,0},{2,3},{3,2},{4,5},{5,4},{6,7},{7,6},{8,9},{9,8},{10,11... | collective-permute-start | bytes 1216520 | tf_op jit(solution)/shard_map/ppermute | solution.py:330
  40.0 1.6 %collective-permute-done.5.refs_2_ = bf16[528,384]{1,0:T(8,128)(2,1)S(1)} collective-permute-done((bf16[528,384]{1,0:T(8,128)(2,1)S(1)}, bf16[528,384]{1,0:T(8,128)(2,1)S(1)}, u32[]{:S(2)}, u32[]{:S(2)}) %collective-permute-start.5) | collective-permute-done | bytes 405536 | tf_op jit(solution)/shard_map/ppermute | solution.py:329
  41.6 1.4 %collective-permute-start.6 = (bf16[528,384]{1,0:T(8,128)(2,1)S(1)}, bf16[528,384]{1,0:T(8,128)(2,1)S(1)}, u32[]{:S(2)}, u32[]{:S(2)}) collective-permute-start(bf16[528,384]{1,0:T(8,128)(2,1)S(1)} %collective-permute-done.5.refs_2_), channel_id=1, source_target_pairs={{0,1},{1,0},{2,3},{3,2},{4,5},{5,4},{6,7},{7,6},{8,9},{9,8},{10,11... | collective-permute-start | bytes 1216520 | tf_op jit(solution)/shard_map/ppermute | solution.py:330
  43.0 1.4 %collective-permute-done.6.refs_3_ = bf16[528,384]{1,0:T(8,128)(2,1)S(1)} collective-permute-done((bf16[528,384]{1,0:T(8,128)(2,1)S(1)}, bf16[528,384]{1,0:T(8,128)(2,1)S(1)}, u32[]{:S(2)}, u32[]{:S(2)}) %collective-permute-start.6) | collective-permute-done | bytes 405536 | tf_op jit(solution)/shard_map/ppermute | solution.py:330
  44.3 3.8 %shard_map.78 = f32[8,256]{1,0:T(8,128)S(1)} custom-call(s32[3]{0:T(128)S(1)} %pad_add_fusion.place, bf16[528,384]{1,0:T(8,128)(2,1)S(1)} %shard_map.77.refs_0_, bf16[528,384]{1,0:T(8,128)(2,1)S(1)} %collective-permute-done.4.refs_1_, bf16[528,384]{1,0:T(8,128)(2,1)S(1)} %collective-permute-done.5.refs_2_, ...), custom_call_target="tpu_custom_call" | custom-call | tf_op jit(solution)/shard_map/pallas_call | solution.py:335
  48.1 0.8 collective-permute-start.11
  48.9 0.8 collective-permute-done.11
  49.8 6.2 %collective-permute-start.14 = (f32[16,256]{1,0:T(8,128)S(1)}, f32[16,256]{1,0:T(8,128)S(1)}, u32[]{:S(2)}, u32[]{:S(2)}) collective-permute-start(f32[16,256]{1,0:T(8,128)S(1)} %pad_maximum_fusion.refs_8_), channel_id=1, source_target_pairs={{0,192},{1,193},{2,194},{3,195},{4,196},{5,197},{6,198},{7,199},{8... | collective-permute-start | bytes 49160 | tf_op jit(solution)/shard_map/ppermute | solution.py:349
  56.0 0.9 collective-permute-start.12
  57.4 3.8 %collective-permute-done.13.refs_10_ = f32[16,256]{1,0:T(8,128)S(1)} collective-permute-done((f32[16,256]{1,0:T(8,128)S(1)}, f32[16,256]{1,0:T(8,128)S(1)}, u32[]{:S(2)}, u32[]{:S(2)}) %collective-permute-start.13) | collective-permute-done | bytes 16416 | tf_op jit(solution)/shard_map/ppermute | solution.py:349
  61.2 15.0 %shard_map.79 = (bf16[144,128]{1,0:T(8,128)(2,1)S(1)}, bf16[144,128]{1,0:T(8,128)(2,1)S(1)}, bf16[144,128]{1,0:T(8,128)(2,1)S(1)}, bf16[144,128]{1,0:T(8,128)(2,1)S(1)}) custom-call(s32[3]{0:T(128)S(1)} %pad_add_fusion.place, bf16[528,384]{1,0:T(8,128)(2,1)S(1)} %shard_map.77.refs_0_, bf16[528,384]{1,0:T(8,128)(2,1)S(1)} %collective-permute-done.4.refs_1_, ...), custom_call_target="tpu_custom_call" | custom-call | tf_op jit(solution)/shard_map/pallas_call | solution.py:350
  77.0 2.0 %collective-permute-start.17 = (bf16[144,128]{1,0:T(8,128)(2,1)S(1)}, bf16[144,128]{1,0:T(8,128)(2,1)S(1)}, u32[]{:S(2)}, u32[]{:S(2)}) collective-permute-start(bf16[144,128]{1,0:T(8,128)(2,1)S(1)} %get-tuple-element.20), channel_id=1, source_target_pairs={{16,0},{48,1},{18,2},{50,3},{20,4},{52,5},{22,6},{54,7},{24,8},{56... | collective-permute-start | bytes 110600 | tf_op jit(solution)/shard_map/ppermute | solution.py:364
  79.0 2.8 %collective-permute-start.18 = (bf16[144,128]{1,0:T(8,128)(2,1)S(1)}, bf16[144,128]{1,0:T(8,128)(2,1)S(1)}, u32[]{:S(2)}, u32[]{:S(2)}) collective-permute-start(bf16[144,128]{1,0:T(8,128)(2,1)S(1)} %get-tuple-element.21), channel_id=1, source_target_pairs={{24,0},{56,1},{26,2},{58,3},{28,4},{60,5},{30,6},{62,7},{0,8},{32,... | collective-permute-start | bytes 110600 | tf_op jit(solution)/shard_map/ppermute | solution.py:364
  82.0 1.5 %collective-permute-done.18.g3 = bf16[144,128]{1,0:T(8,128)(2,1)S(1)} collective-permute-done((bf16[144,128]{1,0:T(8,128)(2,1)S(1)}, bf16[144,128]{1,0:T(8,128)(2,1)S(1)}, u32[]{:S(2)}, u32[]{:S(2)}) %collective-permute-start.18) | collective-permute-done | bytes 36896 | tf_op jit(solution)/shard_map/ppermute | solution.py:364
  83.5 1.2 %shard_map.80 = (bf16[128,256]{1,0:T(8,128)(2,1)}, bf16[128,256]{1,0:T(8,128)(2,1)}, f32[8,128]{1,0:T(8,128)S(1)}) custom-call(s32[3]{0:T(128)S(1)} %pad_add_fusion.place, bf16[144,128]{1,0:T(8,128)(2,1)S(1)} %collective-permute-done.15.g0, bf16[144,128]{1,0:T(8,128)(2,1)S(1)} %collective-permute-done.16.g1, ...), custom_call_target="tpu_custom_call" | custom-call | tf_op jit(solution)/shard_map/pallas_call | solution.py:366
  84.7 0.9 collective-permute-start.19
  85.6 2.7 %collective-permute-done.19 = f32[8,128]{1,0:T(8,128)S(1)} collective-permute-done((f32[8,128]{1,0:T(8,128)S(1)}, f32[8,128]{1,0:T(8,128)S(1)}, u32[]{:S(2)}, u32[]{:S(2)}) %collective-permute-start.19) | collective-permute-done | bytes 4128 | tf_op jit(solution)/shard_map/ppermute | solution.py:375
  88.3 2.5 %collective-permute-start.20 = (f32[8,128]{1,0:T(8,128)S(1)}, f32[8,128]{1,0:T(8,128)S(1)}, u32[]{:S(2)}, u32[]{:S(2)}) collective-permute-start(f32[8,128]{1,0:T(8,128)S(1)} %add.19), channel_id=1, source_target_pairs={{0,4},{1,5},{2,6},{3,7},{4,0},{5,1},{6,2},{7,3},{8,12},{9,13},{10,... | collective-permute-start | bytes 12296 | tf_op jit(solution)/shard_map/ppermute | solution.py:375
  90.8 2.7 %collective-permute-done.20 = f32[8,128]{1,0:T(8,128)S(1)} collective-permute-done((f32[8,128]{1,0:T(8,128)S(1)}, f32[8,128]{1,0:T(8,128)S(1)}, u32[]{:S(2)}, u32[]{:S(2)}) %collective-permute-start.20) | collective-permute-done | bytes 4128 | tf_op jit(solution)/shard_map/ppermute | solution.py:375
  93.4 9.0 %collective-permute-start.21 = (f32[8,128]{1,0:T(8,128)S(1)}, f32[8,128]{1,0:T(8,128)S(1)}, u32[]{:S(2)}, u32[]{:S(2)}) collective-permute-start(f32[8,128]{1,0:T(8,128)S(1)} %add.20), channel_id=1, source_target_pairs={{0,1},{1,0},{2,3},{3,2},{4,5},{5,4},{6,7},{7,6},{8,9},{9,8},{10,11... | collective-permute-start | bytes 12296 | tf_op jit(solution)/shard_map/ppermute | solution.py:375
  102.4 0.8 collective-permute-done.21
  (32 shorter events, 5.5 us)
Async XLA Ops:
  0.6 0.8 copy-start.2
  0.7 0.7 copy-start.4
  1.5 0.9 copy-start
  2.4 0.9 copy-start.1
  3.3 0.8 copy-start.3
  4.9 6.1 %collective-permute-start = (bf16[144,384]{1,0:T(8,128)(2,1)S(1)}, bf16[144,384]{1,0:T(8,128)(2,1)S(1)}, u32[]{:S(2)}, u32[]{:S(2)}) collective-permute-start(bf16[144,384]{1,0:T(8,128)(2,1)S(1)} %get-tuple-element.14), channel_id=1, source_target_pairs={{0,0},{1,32},{2,2},{3,34},{4,4},{5,36},{6,6},{7,38},{8,8},{9,40},{... | collective-permute-start | bytes 331784 | tf_op jit(solution)/shard_map/ppermute | solution.py:319
  5.5 5.4 %collective-permute-start.1 = (bf16[144,384]{1,0:T(8,128)(2,1)S(1)}, bf16[144,384]{1,0:T(8,128)(2,1)S(1)}, u32[]{:S(2)}, u32[]{:S(2)}) collective-permute-start(bf16[144,384]{1,0:T(8,128)(2,1)S(1)} %get-tuple-element.15), channel_id=1, source_target_pairs={{0,8},{1,40},{2,10},{3,42},{4,12},{5,44},{6,14},{7,46},{8,16},{9,4... | collective-permute-start | bytes 331784 | tf_op jit(solution)/shard_map/ppermute | solution.py:319
  7.5 9.3 %collective-permute-start.2 = (bf16[144,384]{1,0:T(8,128)(2,1)S(1)}, bf16[144,384]{1,0:T(8,128)(2,1)S(1)}, u32[]{:S(2)}, u32[]{:S(2)}) collective-permute-start(bf16[144,384]{1,0:T(8,128)(2,1)S(1)} %get-tuple-element.16), channel_id=1, source_target_pairs={{0,16},{1,48},{2,18},{3,50},{4,20},{5,52},{6,22},{7,54},{8,24},{9,... | collective-permute-start | bytes 331784 | tf_op jit(solution)/shard_map/ppermute | solution.py:319
  9.8 8.7 %collective-permute-start.3 = (bf16[144,384]{1,0:T(8,128)(2,1)S(1)}, bf16[144,384]{1,0:T(8,128)(2,1)S(1)}, u32[]{:S(2)}, u32[]{:S(2)}) collective-permute-start(bf16[144,384]{1,0:T(8,128)(2,1)S(1)} %get-tuple-element.17), channel_id=1, source_target_pairs={{0,24},{1,56},{2,26},{3,58},{4,28},{5,60},{6,30},{7,62},{8,0},{9,3... | collective-permute-start | bytes 331784 | tf_op jit(solution)/shard_map/ppermute | solution.py:319
  19.1 9.4 %collective-permute-start.9 = (bf16[528,384]{1,0:T(8,128)(2,1)S(1)}, bf16[528,384]{1,0:T(8,128)(2,1)S(1)}, u32[]{:S(2)}, u32[]{:S(2)}) collective-permute-start(bf16[528,384]{1,0:T(8,128)(2,1)S(1)} %shard_map.77.refs_0_), channel_id=1, source_target_pairs={{0,192},{1,193},{2,194},{3,195},{4,196},{5,197},{6,198},{7,199},{8... | collective-permute-start | bytes 1216520 | tf_op jit(solution)/shard_map/ppermute | solution.py:329
  20.7 19.3 %collective-permute-start.7 = (bf16[528,384]{1,0:T(8,128)(2,1)S(1)}, bf16[528,384]{1,0:T(8,128)(2,1)S(1)}, u32[]{:S(2)}, u32[]{:S(2)}) collective-permute-start(bf16[528,384]{1,0:T(8,128)(2,1)S(1)} %shard_map.77.refs_0_), channel_id=1, source_target_pairs={{0,128},{1,129},{2,130},{3,131},{4,132},{5,133},{6,134},{7,135},{8... | collective-permute-start | bytes 1216520 | tf_op jit(solution)/shard_map/ppermute | solution.py:329
  21.3 20.3 %collective-permute-start.5 = (bf16[528,384]{1,0:T(8,128)(2,1)S(1)}, bf16[528,384]{1,0:T(8,128)(2,1)S(1)}, u32[]{:S(2)}, u32[]{:S(2)}) collective-permute-start(bf16[528,384]{1,0:T(8,128)(2,1)S(1)} %shard_map.77.refs_0_), channel_id=1, source_target_pairs={{0,64},{1,65},{2,66},{3,67},{4,68},{5,69},{6,70},{7,71},{8,72},{9,... | collective-permute-start | bytes 1216520 | tf_op jit(solution)/shard_map/ppermute | solution.py:329
  22.3 20.7 %collective-permute-start.4 = (bf16[528,384]{1,0:T(8,128)(2,1)S(1)}, bf16[528,384]{1,0:T(8,128)(2,1)S(1)}, u32[]{:S(2)}, u32[]{:S(2)}) collective-permute-start(bf16[528,384]{1,0:T(8,128)(2,1)S(1)} %shard_map.77.refs_0_), channel_id=1, source_target_pairs={{0,1},{1,0},{2,3},{3,2},{4,5},{5,4},{6,7},{7,6},{8,9},{9,8},{10,11... | collective-permute-start | bytes 1216520 | tf_op jit(solution)/shard_map/ppermute | solution.py:330
  28.5 14.5 %collective-permute-start.10 = (bf16[528,384]{1,0:T(8,128)(2,1)S(1)}, bf16[528,384]{1,0:T(8,128)(2,1)S(1)}, u32[]{:S(2)}, u32[]{:S(2)}) collective-permute-start(bf16[528,384]{1,0:T(8,128)(2,1)S(1)} %collective-permute-done.9.refs_6_), channel_id=1, source_target_pairs={{0,1},{1,0},{2,3},{3,2},{4,5},{5,4},{6,7},{7,6},{8,9},{9,8},{10,11... | collective-permute-start | bytes 1216520 | tf_op jit(solution)/shard_map/ppermute | solution.py:330
  40.0 3.0 %collective-permute-start.8 = (bf16[528,384]{1,0:T(8,128)(2,1)S(1)}, bf16[528,384]{1,0:T(8,128)(2,1)S(1)}, u32[]{:S(2)}, u32[]{:S(2)}) collective-permute-start(bf16[528,384]{1,0:T(8,128)(2,1)S(1)} %collective-permute-done.7.refs_4_), channel_id=1, source_target_pairs={{0,1},{1,0},{2,3},{3,2},{4,5},{5,4},{6,7},{7,6},{8,9},{9,8},{10,11... | collective-permute-start | bytes 1216520 | tf_op jit(solution)/shard_map/ppermute | solution.py:330
  41.6 2.8 %collective-permute-start.6 = (bf16[528,384]{1,0:T(8,128)(2,1)S(1)}, bf16[528,384]{1,0:T(8,128)(2,1)S(1)}, u32[]{:S(2)}, u32[]{:S(2)}) collective-permute-start(bf16[528,384]{1,0:T(8,128)(2,1)S(1)} %collective-permute-done.5.refs_2_), channel_id=1, source_target_pairs={{0,1},{1,0},{2,3},{3,2},{4,5},{5,4},{6,7},{7,6},{8,9},{9,8},{10,11... | collective-permute-start | bytes 1216520 | tf_op jit(solution)/shard_map/ppermute | solution.py:330
  48.1 1.7 %collective-permute-start.11 = (f32[8,256]{1,0:T(8,128)S(1)}, f32[8,256]{1,0:T(8,128)S(1)}, u32[]{:S(2)}, u32[]{:S(2)}) collective-permute-start(f32[8,256]{1,0:T(8,128)S(1)} %shard_map.78), channel_id=1, source_target_pairs={{0,1},{1,0},{2,3},{3,2},{4,5},{5,4},{6,7},{7,6},{8,9},{9,8},{10,11... | collective-permute-start | bytes 24584 | tf_op jit(solution)/shard_map/ppermute | solution.py:348
  49.8 7.7 %collective-permute-start.14 = (f32[16,256]{1,0:T(8,128)S(1)}, f32[16,256]{1,0:T(8,128)S(1)}, u32[]{:S(2)}, u32[]{:S(2)}) collective-permute-start(f32[16,256]{1,0:T(8,128)S(1)} %pad_maximum_fusion.refs_8_), channel_id=1, source_target_pairs={{0,192},{1,193},{2,194},{3,195},{4,196},{5,197},{6,198},{7,199},{8... | collective-permute-start | bytes 49160 | tf_op jit(solution)/shard_map/ppermute | solution.py:349
  56.0 5.2 %collective-permute-start.13 = (f32[16,256]{1,0:T(8,128)S(1)}, f32[16,256]{1,0:T(8,128)S(1)}, u32[]{:S(2)}, u32[]{:S(2)}) collective-permute-start(f32[16,256]{1,0:T(8,128)S(1)} %pad_maximum_fusion.refs_8_), channel_id=1, source_target_pairs={{0,128},{1,129},{2,130},{3,131},{4,132},{5,133},{6,134},{7,135},{8... | collective-permute-start | bytes 49160 | tf_op jit(solution)/shard_map/ppermute | solution.py:349
  56.0 5.2 %collective-permute-start.12 = (f32[16,256]{1,0:T(8,128)S(1)}, f32[16,256]{1,0:T(8,128)S(1)}, u32[]{:S(2)}, u32[]{:S(2)}) collective-permute-start(f32[16,256]{1,0:T(8,128)S(1)} %pad_maximum_fusion.refs_8_), channel_id=1, source_target_pairs={{0,64},{1,65},{2,66},{3,67},{4,68},{5,69},{6,70},{7,71},{8,72},{9,... | collective-permute-start | bytes 49160 | tf_op jit(solution)/shard_map/ppermute | solution.py:349
  76.2 5.6 %collective-permute-start.15 = (bf16[144,128]{1,0:T(8,128)(2,1)S(1)}, bf16[144,128]{1,0:T(8,128)(2,1)S(1)}, u32[]{:S(2)}, u32[]{:S(2)}) collective-permute-start(bf16[144,128]{1,0:T(8,128)(2,1)S(1)} %get-tuple-element.18), channel_id=1, source_target_pairs={{0,0},{32,1},{2,2},{34,3},{4,4},{36,5},{6,6},{38,7},{8,8},{40,9},{... | collective-permute-start | bytes 110600 | tf_op jit(solution)/shard_map/ppermute | solution.py:364
  76.9 4.9 %collective-permute-start.16 = (bf16[144,128]{1,0:T(8,128)(2,1)S(1)}, bf16[144,128]{1,0:T(8,128)(2,1)S(1)}, u32[]{:S(2)}, u32[]{:S(2)}) collective-permute-start(bf16[144,128]{1,0:T(8,128)(2,1)S(1)} %get-tuple-element.19), channel_id=1, source_target_pairs={{8,0},{40,1},{10,2},{42,3},{12,4},{44,5},{14,6},{46,7},{16,8},{48,... | collective-permute-start | bytes 110600 | tf_op jit(solution)/shard_map/ppermute | solution.py:364
  77.0 4.9 %collective-permute-start.17 = (bf16[144,128]{1,0:T(8,128)(2,1)S(1)}, bf16[144,128]{1,0:T(8,128)(2,1)S(1)}, u32[]{:S(2)}, u32[]{:S(2)}) collective-permute-start(bf16[144,128]{1,0:T(8,128)(2,1)S(1)} %get-tuple-element.20), channel_id=1, source_target_pairs={{16,0},{48,1},{18,2},{50,3},{20,4},{52,5},{22,6},{54,7},{24,8},{56... | collective-permute-start | bytes 110600 | tf_op jit(solution)/shard_map/ppermute | solution.py:364
  79.0 4.5 %collective-permute-start.18 = (bf16[144,128]{1,0:T(8,128)(2,1)S(1)}, bf16[144,128]{1,0:T(8,128)(2,1)S(1)}, u32[]{:S(2)}, u32[]{:S(2)}) collective-permute-start(bf16[144,128]{1,0:T(8,128)(2,1)S(1)} %get-tuple-element.21), channel_id=1, source_target_pairs={{24,0},{56,1},{26,2},{58,3},{28,4},{60,5},{30,6},{62,7},{0,8},{32,... | collective-permute-start | bytes 110600 | tf_op jit(solution)/shard_map/ppermute | solution.py:364
  84.7 3.6 %collective-permute-start.19 = (f32[8,128]{1,0:T(8,128)S(1)}, f32[8,128]{1,0:T(8,128)S(1)}, u32[]{:S(2)}, u32[]{:S(2)}) collective-permute-start(f32[8,128]{1,0:T(8,128)S(1)} %get-tuple-element.22), channel_id=1, source_target_pairs={{0,2},{1,3},{2,0},{3,1},{4,6},{5,7},{6,4},{7,5},{8,10},{9,11},{10,... | collective-permute-start | bytes 12296 | tf_op jit(solution)/shard_map/ppermute | solution.py:375
  88.3 5.1 %collective-permute-start.20 = (f32[8,128]{1,0:T(8,128)S(1)}, f32[8,128]{1,0:T(8,128)S(1)}, u32[]{:S(2)}, u32[]{:S(2)}) collective-permute-start(f32[8,128]{1,0:T(8,128)S(1)} %add.19), channel_id=1, source_target_pairs={{0,4},{1,5},{2,6},{3,7},{4,0},{5,1},{6,2},{7,3},{8,12},{9,13},{10,... | collective-permute-start | bytes 12296 | tf_op jit(solution)/shard_map/ppermute | solution.py:375
  93.4 9.8 %collective-permute-start.21 = (f32[8,128]{1,0:T(8,128)S(1)}, f32[8,128]{1,0:T(8,128)S(1)}, u32[]{:S(2)}, u32[]{:S(2)}) collective-permute-start(f32[8,128]{1,0:T(8,128)S(1)} %add.20), channel_id=1, source_target_pairs={{0,1},{1,0},{2,3},{3,2},{4,5},{5,4},{6,7},{7,6},{8,9},{9,8},{10,11... | collective-permute-start | bytes 12296 | tf_op jit(solution)/shard_map/ppermute | solution.py:375
